TPU v7x, 32 devices: a whole 2x2x4 slice. The times are simulated.
32 devices in a mesh: section: 4 (over y, x), dp: 2 (over core), expert: 4 (over z).
Axes of the slice: x: 2, y: 2, z: 4, core: 2. Of those that a mesh axis runs over, the one named last changes fastest.
Arguments:
- tokens: bfloat16 [8192, 384], P(('section', 'dp', 'expert')), may hold values from -6 to 6
- timesteps: int32 [32], P(('section', 'dp', 'expert')), may hold values from 0 to 999
- routes_one: int32 [8192, 2], P(('section', 'dp', 'expert')), may hold values from 0 to 3, all different within a row; in each aligned block of 256 rows (0 to 255, 256 to 511, ...) at most 256 rows name the same one
- routes_two: int32 [8192, 2], P(('section', 'dp', 'expert')), may hold values from 0 to 3, all different within a row; in each aligned block of 256 rows (0 to 255, 256 to 511, ...) at most 256 rows name the same one
- cotangent: bfloat16 [8192, 384], P(('section', 'dp', 'expert')), may hold values from -6 to 6
- time_table: bfloat16 [1000, 384], replicated, may hold values from -6 to 6
- ada_weight: bfloat16 [4, 384, 1152], P('section'), may hold values from -0.3125 to 0.3125
- ada_bias: bfloat16 [4, 1152], P('section'), may hold values from -4 to 4
- qkv_weight: bfloat16 [2, 384, 1152], replicated, may hold values from -0.3125 to 0.3125
- qv_bias: bfloat16 [2, 768], replicated, may hold values from -3 to 3
- out_weight: bfloat16 [2, 384, 384], replicated, may hold values from -2.5 to 2.5
- out_bias: bfloat16 [2, 384], replicated, may hold values from -3 to 3
- router_weight: bfloat16 [2, 384, 4], replicated, may hold values from -0.21875 to 0.21875
- shared_up: bfloat16 [2, 384, 3072], replicated, may hold values from -0.3125 to 0.3125
- shared_up_bias: bfloat16 [2, 3072], replicated, may hold values from -3 to 3
- shared_down: bfloat16 [2, 3072, 384], replicated, may hold values from -0.109375 to 0.109375
- shared_down_bias: bfloat16 [2, 384], replicated, may hold values from -3 to 3
- expert_up: bfloat16 [2, 4, 384, 1536], P(None, 'expert'), may hold values from -0.3125 to 0.3125
- expert_up_bias: bfloat16 [2, 4, 1536], P(None, 'expert'), may hold values from -3 to 3
- expert_down: bfloat16 [2, 4, 1536, 384], P(None, 'expert'), may hold values from -0.15625 to 0.15625
- expert_down_bias: bfloat16 [2, 4, 384], P(None, 'expert'), may hold values from -3 to 3
Outputs:
- output: bfloat16 [8192, 384], P(('section', 'dp', 'expert'))
- grad_tokens: float32 [8192, 384], P(('section', 'dp', 'expert'))
- grad_time_table: float32 [1000, 384], replicated
- grad_ada_weight: float32 [4, 384, 1152], P('section')
- grad_ada_bias: float32 [4, 1152], P('section')
- grad_qkv_weight: float32 [2, 384, 1152], replicated
- grad_qv_bias: float32 [2, 768], replicated
- grad_out_weight: float32 [2, 384, 384], replicated
- grad_out_bias: float32 [2, 384], replicated
- grad_router_weight: float32 [2, 384, 4], replicated
- grad_shared_up: float32 [2, 384, 3072], replicated
- grad_shared_up_bias: float32 [2, 3072], replicated
- grad_shared_down: float32 [2, 3072, 384], replicated
- grad_shared_down_bias: float32 [2, 384], replicated
- grad_expert_up: float32 [2, 4, 384, 1536], P(None, 'expert')
- grad_expert_up_bias: float32 [2, 4, 1536], P(None, 'expert')
- grad_expert_down: float32 [2, 4, 1536, 384], P(None, 'expert')
- grad_expert_down_bias: float32 [2, 4, 384], P(None, 'expert')
- counts: int32 [2, 4], replicated
Inputs may be any that keep to these rules, and one draw needn't show every extreme that they name: `routes_one`: in each aligned block of 256 rows (one device's tokens), no expert is named more than 256 times. `routes_two`: in each aligned block of 256 rows (one device's tokens), no expert is named more than 256 times.
All inputs are finite; a program needn't handle non-finite values.
Results may differ from a plain program's by a relative error of at most 0.039.
Values may be sent and summed in bfloat16 or wider, within the bound.
No kernel may reach another device: no remote copies, remote signals or barrier semaphores. Data moves between devices by JAX's collectives and lax.ppermute only.
A program may use at most 256 MiB of HBM per device.

v0:
```python
import jax
import jax.numpy as jnp
from jax import lax
from jax.sharding import PartitionSpec as P

HEADS = 6
HD = 64
PATCHES = 256


HIGHEST_PRECISION = lax.Precision.HIGHEST
BFLOAT = jnp.bfloat16
FLOAT = jnp.float32


def from_behind(x, axis, by):
    devices = lax.axis_size(axis)
    pairs = [(i, i + by) for i in range(devices) if 0 <= i + by < devices]
    return lax.ppermute(x, axis, pairs)


def exact_product(left_arg, right_arg):
    return jnp.dot(left_arg, right_arg, precision=HIGHEST_PRECISION, preferred_element_type=FLOAT)


def plain_product(left_arg, right_arg):
    return jnp.dot(left_arg, right_arg, preferred_element_type=FLOAT)


def lead_product(left_arg, right_arg):
    return lax.dot_general(
        left_arg, right_arg, (((0,), (0,)), ((), ())), preferred_element_type=FLOAT
    )


def lead_exact(left_arg, right_arg):
    return lax.dot_general(
        left_arg,
        right_arg,
        (((0,), (0,)), ((), ())),
        precision=HIGHEST_PRECISION,
        preferred_element_type=FLOAT,
    )


def back_product(left_arg, right_arg):
    return lax.dot_general(
        left_arg, right_arg, (((1,), (1,)), ((), ())), preferred_element_type=FLOAT
    )


def back_exact(left_arg, right_arg):
    return lax.dot_general(
        left_arg,
        right_arg,
        (((1,), (1,)), ((), ())),
        precision=HIGHEST_PRECISION,
        preferred_element_type=FLOAT,
    )


def gelu_tanh(inputs_pre):
    return jax.nn.gelu(inputs_pre, approximate=True)


def gelu_grad(inputs_pre, upstream):
    return jax.vjp(gelu_tanh, inputs_pre)[1](upstream)[0]


def normalize(stream, shifts, scaling):
    row_mean = jnp.mean(stream, -1, keepdims=True)
    centred = stream - row_mean
    variance = jnp.mean(centred * centred, -1, keepdims=True)
    return centred * lax.rsqrt(variance + 1e-06) * (1.0 + scaling) + shifts


def split_modulation(token_mod, model_width):
    return (
        token_mod[:, :model_width],
        token_mod[:, model_width : 2 * model_width],
        token_mod[:, 2 * model_width :],
    )


def store(buffer, value, position, is_valid):
    current = lax.dynamic_index_in_dim(buffer, position, 0, keepdims=False)
    return lax.dynamic_update_index_in_dim(buffer, jnp.where(is_valid, value, current), position, 0)


def row_pick(buffer, position):
    return lax.dynamic_index_in_dim(buffer, position, 0, keepdims=False)


def slot_numbers(route_pair, experts_total, capacity):
    flat_routes = route_pair.reshape(-1)
    route_marks = (
        flat_routes[:, None] == jnp.arange(experts_total, dtype=jnp.int32)[None, :]
    ).astype(jnp.int32)
    before = jnp.cumsum(route_marks, 0) - route_marks
    return flat_routes * capacity + jnp.sum(before * route_marks, 1)


def pack_rows(per_slot, slot_index, devices, local_experts, capacity):
    model_width = per_slot.shape[1]
    buffer = (
        jnp.zeros((devices * local_experts * capacity, model_width), per_slot.dtype)
        .at[slot_index]
        .set(per_slot)
    )
    return buffer.reshape(devices, local_experts, capacity, model_width)


def attention_forward(stream, token_mod, attn_weights):
    qkv_matrix, qv_offset, out_matrix, out_offset = attn_weights
    model_width = stream.shape[1]
    shifts, scaling, gating = split_modulation(token_mod, model_width)
    hidden = normalize(stream, shifts, scaling).astype(BFLOAT)
    projected = plain_product(hidden, qkv_matrix)
    images = stream.shape[0] // PATCHES

    def heads_view(rows):
        return rows.astype(BFLOAT).reshape(images, PATCHES, HEADS, HD)

    query_rows = heads_view(projected[:, :model_width] + qv_offset[:model_width])
    key_rows = heads_view(projected[:, model_width : 2 * model_width])
    value_rows = heads_view(projected[:, 2 * model_width :] + qv_offset[model_width:])
    scores = jnp.einsum(
        "iqhd,ikhd->ihqk", query_rows, key_rows, preferred_element_type=FLOAT
    ) * HD ** (-0.5)
    weights_soft = jax.nn.softmax(scores, -1)
    probs_low = weights_soft.astype(BFLOAT)
    attended = (
        jnp.einsum("ihqk,ikhd->iqhd", probs_low, value_rows, preferred_element_type=FLOAT)
        .reshape(-1, model_width)
        .astype(BFLOAT)
    )
    branch = plain_product(attended, out_matrix) + out_offset
    pieces = (
        hidden,
        query_rows,
        key_rows,
        value_rows,
        weights_soft,
        probs_low,
        attended,
        branch,
        gating,
        shifts,
        scaling,
    )
    return (stream + gating * branch, pieces)


def attention_backward(stream, token_mod, attn_weights, upstream):
    qkv_matrix, qv_offset, out_matrix, out_offset = attn_weights
    new_stream, pieces = attention_forward(stream, token_mod, attn_weights)
    (
        hidden,
        query_rows,
        key_rows,
        value_rows,
        weights_soft,
        probs_low,
        attended,
        branch,
        gating,
        shifts,
        scaling,
    ) = pieces
    model_width = stream.shape[1]
    factor = HD ** (-0.5)
    gate_grad = upstream * branch
    branch_grad = (gating * upstream).astype(BFLOAT)
    outw_grad = lead_product(attended, branch_grad)
    outb_grad = jnp.sum(branch_grad.astype(FLOAT), 0)
    attended_grad = back_product(branch_grad, out_matrix).astype(BFLOAT).reshape(query_rows.shape)
    value_grad = jnp.einsum(
        "ihqk,iqhd->ikhd", probs_low, attended_grad, preferred_element_type=FLOAT
    )
    prob_grad = jnp.einsum(
        "iqhd,ikhd->ihqk", attended_grad, value_rows, preferred_element_type=FLOAT
    )
    score_grad = (
        weights_soft * (prob_grad - jnp.sum(prob_grad * weights_soft, -1, keepdims=True))
    ).astype(BFLOAT)
    query_grad = (
        jnp.einsum("ihqk,ikhd->iqhd", score_grad, key_rows, preferred_element_type=FLOAT) * factor
    )
    key_grad = (
        jnp.einsum("ihqk,iqhd->ikhd", score_grad, query_rows, preferred_element_type=FLOAT) * factor
    )
    proj_grad = jnp.concatenate(
        [
            query_grad.reshape(-1, model_width),
            key_grad.reshape(-1, model_width),
            value_grad.reshape(-1, model_width),
        ],
        -1,
    ).astype(BFLOAT)
    qkv_grad = lead_product(hidden, proj_grad)
    proj_float = proj_grad.astype(FLOAT)
    offset_grad = jnp.concatenate(
        [jnp.sum(proj_float[:, :model_width], 0), jnp.sum(proj_float[:, 2 * model_width :], 0)]
    )
    hidden_grad = back_product(proj_grad, qkv_matrix)
    pullback = jax.vjp(normalize, stream, shifts, scaling)[1]
    stream_grad, shift_grad, scale_grad = pullback(hidden_grad)
    mod_grad = jnp.concatenate([shift_grad, scale_grad, gate_grad], -1)
    return (stream_grad + upstream, mod_grad, (qkv_grad, offset_grad, outw_grad, outb_grad))


def experts_forward(stream, token_mod, moe_weights, route_pair):
    (
        router_matrix,
        shared_upper,
        shared_upbias,
        shared_lower,
        shared_lowbias,
        expert_upper,
        expert_upbias,
        expert_lower,
        expert_lowbias,
    ) = moe_weights
    model_width = stream.shape[1]
    shifts, scaling, gating = split_modulation(token_mod, model_width)
    hidden = normalize(stream, shifts, scaling).astype(BFLOAT)
    logits = exact_product(hidden.astype(FLOAT), router_matrix)
    gate_probs = jax.nn.softmax(jnp.take_along_axis(logits, route_pair, 1), -1)
    shared_pre = plain_product(hidden, shared_upper) + shared_upbias
    shared_act = gelu_tanh(shared_pre).astype(BFLOAT)
    shared_out = plain_product(shared_act, shared_lower) + shared_lowbias
    devices = lax.axis_size("expert")
    local_experts = expert_upper.shape[0]
    experts_total = devices * local_experts
    capacity = 4 * stream.shape[0] // experts_total
    slot_index = slot_numbers(route_pair, experts_total, capacity)
    packed = pack_rows(jnp.repeat(hidden, 2, axis=0), slot_index, devices, local_experts, capacity)
    expert_rows = lax.all_to_all(packed, "expert", split_axis=0, concat_axis=2, tiled=True).reshape(
        local_experts, devices * capacity, model_width
    )
    expert_pre = (
        jnp.einsum("erd,edf->erf", expert_rows, expert_upper, preferred_element_type=FLOAT)
        + expert_upbias[:, None, :]
    )
    expert_act = gelu_tanh(expert_pre).astype(BFLOAT)
    expert_out = (
        jnp.einsum("erf,efd->erd", expert_act, expert_lower, preferred_element_type=FLOAT)
        + expert_lowbias[:, None, :]
    ).astype(BFLOAT)
    coming = lax.all_to_all(
        expert_out.reshape(1, local_experts, devices * capacity, model_width),
        "expert",
        split_axis=2,
        concat_axis=0,
        tiled=True,
    )
    returned = jnp.take(coming.reshape(-1, model_width), slot_index, axis=0).reshape(
        -1, 2, model_width
    )
    routed = jnp.sum(gate_probs[:, :, None] * returned.astype(FLOAT), 1)
    branch = shared_out + routed
    pieces = (
        hidden,
        gating,
        gate_probs,
        shared_pre,
        shared_act,
        slot_index,
        expert_rows,
        expert_pre,
        expert_act,
        returned,
        branch,
        shifts,
        scaling,
    )
    return (stream + gating * branch, pieces)


def experts_backward(stream, token_mod, moe_weights, route_pair, upstream):
    (
        router_matrix,
        shared_upper,
        shared_upbias,
        shared_lower,
        shared_lowbias,
        expert_upper,
        expert_upbias,
        expert_lower,
        expert_lowbias,
    ) = moe_weights
    new_stream, pieces = experts_forward(stream, token_mod, moe_weights, route_pair)
    (
        hidden,
        gating,
        gate_probs,
        shared_pre,
        shared_act,
        slot_index,
        expert_rows,
        expert_pre,
        expert_act,
        returned,
        branch,
        shifts,
        scaling,
    ) = pieces
    model_width = stream.shape[1]
    devices = lax.axis_size("expert")
    local_experts = expert_upper.shape[0]
    capacity = expert_rows.shape[1] // devices
    gate_grad = upstream * branch
    branch_grad = gating * upstream
    shared_grad = branch_grad.astype(BFLOAT)
    lower_grad = lead_product(shared_act, shared_grad)
    lowbias_grad = jnp.sum(shared_grad.astype(FLOAT), 0)
    shared_pregrad = gelu_grad(shared_pre, back_product(shared_grad, shared_lower)).astype(BFLOAT)
    upper_grad = lead_product(hidden, shared_pregrad)
    upbias_grad = jnp.sum(shared_pregrad.astype(FLOAT), 0)
    hidden_grad = back_product(shared_pregrad, shared_upper)
    prob_grad = jnp.sum(branch_grad[:, None, :] * returned.astype(FLOAT), -1)
    chosen_grad = gate_probs * (prob_grad - jnp.sum(gate_probs * prob_grad, -1, keepdims=True))
    route_marks = (
        route_pair[:, :, None]
        == jnp.arange(devices * local_experts, dtype=jnp.int32)[None, None, :]
    ).astype(FLOAT)
    logit_grad = jnp.sum(route_marks * chosen_grad[:, :, None], 1)
    router_grad = lead_exact(hidden.astype(FLOAT), logit_grad)
    hidden_grad = hidden_grad + back_exact(logit_grad, router_matrix)
    slot_grad = (
        (gate_probs[:, :, None] * branch_grad[:, None, :]).astype(BFLOAT).reshape(-1, model_width)
    )
    packed = pack_rows(slot_grad, slot_index, devices, local_experts, capacity)
    result_grad = lax.all_to_all(packed, "expert", split_axis=0, concat_axis=2, tiled=True).reshape(
        local_experts, devices * capacity, model_width
    )
    expert_lowgrad = jnp.einsum(
        "erf,erd->efd", expert_act, result_grad, preferred_element_type=FLOAT
    )
    expert_lowbiasgrad = jnp.sum(result_grad.astype(FLOAT), 1)
    expert_pregrad = gelu_grad(
        expert_pre,
        jnp.einsum("erd,efd->erf", result_grad, expert_lower, preferred_element_type=FLOAT),
    ).astype(BFLOAT)
    expert_upgrad = jnp.einsum(
        "erd,erf->edf", expert_rows, expert_pregrad, preferred_element_type=FLOAT
    )
    expert_upbiasgrad = jnp.sum(expert_pregrad.astype(FLOAT), 1)
    rows_grad = jnp.einsum(
        "erf,edf->erd", expert_pregrad, expert_upper, preferred_element_type=FLOAT
    ).astype(BFLOAT)
    coming = lax.all_to_all(
        rows_grad.reshape(1, local_experts, devices * capacity, model_width),
        "expert",
        split_axis=2,
        concat_axis=0,
        tiled=True,
    )
    back_rows = jnp.take(coming.reshape(-1, model_width), slot_index, axis=0).reshape(
        -1, 2, model_width
    )
    hidden_grad = hidden_grad + jnp.sum(back_rows.astype(FLOAT), 1)
    pullback = jax.vjp(normalize, stream, shifts, scaling)[1]
    stream_grad, shift_grad, scale_grad = pullback(hidden_grad)
    mod_grad = jnp.concatenate([shift_grad, scale_grad, gate_grad], -1)
    deltas = (
        router_grad,
        upper_grad,
        upbias_grad,
        lower_grad,
        lowbias_grad,
        expert_upgrad,
        expert_upbiasgrad,
        expert_lowgrad,
        expert_lowbiasgrad,
    )
    return (stream_grad + upstream, mod_grad, deltas)


def accumulate(totals, deltas, is_valid):
    return jax.tree.map(
        lambda running, change: running + jnp.where(is_valid, change, 0.0), totals, deltas
    )


def shards(
    tokens,
    timesteps,
    routes_one,
    routes_two,
    cotangent,
    time_table,
    ada_weight,
    ada_bias,
    qkv_weight,
    qv_bias,
    out_weight,
    out_bias,
    router_weight,
    shared_up,
    shared_up_bias,
    shared_down,
    shared_down_bias,
    expert_up,
    expert_up_bias,
    expert_down,
    expert_down_bias,
):
    sections = lax.axis_size("section")
    section_index = lax.axis_index("section")
    layer_index = section_index // 2
    is_attention = section_index % 2 == 0
    micro_tokens, model_width = tokens.shape
    images_micro = timesteps.shape[0]
    steps_count = time_table.shape[0]
    devices = lax.axis_size("expert")
    local_experts = expert_up.shape[1]
    experts_total = devices * local_experts
    gathered = (
        lax.all_gather(tokens, "section", axis=0, tiled=True),
        lax.all_gather(cotangent, "section", axis=0, tiled=True),
        lax.all_gather(routes_one, "section", axis=0, tiled=True),
        lax.all_gather(routes_two, "section", axis=0, tiled=True),
        lax.all_gather(timesteps, "section", axis=0, tiled=True),
    )
    all_tokens = gathered[0].reshape(sections, micro_tokens, model_width)
    all_cotangent = gathered[1].reshape(sections, micro_tokens, model_width)
    first_routes = gathered[2].reshape(sections, micro_tokens, 2)
    second_routes = gathered[3].reshape(sections, micro_tokens, 2)
    route_pairs = jnp.where(layer_index == 0, first_routes, second_routes)
    pick_rows = (gathered[4][:, None] == jnp.arange(steps_count, dtype=jnp.int32)[None, :]).astype(
        FLOAT
    )
    embedded = exact_product(pick_rows, time_table.astype(FLOAT))
    condition = lax.optimization_barrier(jax.nn.silu(embedded).astype(BFLOAT)).astype(FLOAT)
    ada_matrix = ada_weight[0].astype(FLOAT)
    ada_offset = ada_bias[0].astype(FLOAT)
    modulations = (exact_product(condition, ada_matrix) + ada_offset).reshape(
        sections, images_micro, 3 * model_width
    )
    condition_rows = condition.reshape(sections, images_micro, model_width)
    embedded_rows = embedded.reshape(sections, images_micro, model_width)
    pick_blocks = pick_rows.reshape(sections, images_micro, steps_count)

    def pick_layer(array):
        return lax.dynamic_index_in_dim(array, layer_index, 0, keepdims=False)

    attn_weights = (
        pick_layer(qkv_weight),
        pick_layer(qv_bias).astype(FLOAT),
        pick_layer(out_weight),
        pick_layer(out_bias).astype(FLOAT),
    )
    moe_weights = (
        pick_layer(router_weight).astype(FLOAT),
        pick_layer(shared_up),
        pick_layer(shared_up_bias).astype(FLOAT),
        pick_layer(shared_down),
        pick_layer(shared_down_bias).astype(FLOAT),
        pick_layer(expert_up),
        pick_layer(expert_up_bias).astype(FLOAT),
        pick_layer(expert_down),
        pick_layer(expert_down_bias).astype(FLOAT),
    )

    def micro_inputs(clipped):
        token_mod = jnp.repeat(row_pick(modulations, clipped), PATCHES, axis=0)
        return (token_mod, row_pick(route_pairs, clipped))

    kept_rows = jnp.zeros((1,), BFLOAT)
    kept_returned = jnp.zeros((1,), BFLOAT)

    def attention_branch(operands):
        stream, token_mod, route_pair = operands
        new_stream = attention_forward(stream, token_mod, attn_weights)[0]
        return new_stream

    def experts_branch(operands):
        stream, token_mod, route_pair = operands
        new_stream, pieces = experts_forward(stream, token_mod, moe_weights, route_pair)
        return new_stream

    def forward_tick(tick_index, loop_state):
        incoming, saved_inputs, final_out, rows_store, returned_store = loop_state
        micro_index = tick_index - section_index
        is_valid = (micro_index >= 0) & (micro_index < sections)
        clipped = jnp.clip(micro_index, 0, sections - 1)
        section_input = jnp.where(section_index == 0, row_pick(all_tokens, clipped), incoming)
        saved_inputs = store(saved_inputs, section_input, clipped, is_valid)
        token_mod, route_pair = micro_inputs(clipped)
        outcome = lax.cond(
            is_attention,
            attention_branch,
            experts_branch,
            (section_input.astype(FLOAT), token_mod, route_pair),
        )
        final_out = store(final_out, outcome, clipped, is_valid & (section_index == sections - 1))
        outgoing = from_behind(outcome.astype(BFLOAT), "section", 1)
        return (outgoing, saved_inputs, final_out, rows_store, returned_store)

    start_state = (
        jnp.zeros((micro_tokens, model_width), BFLOAT),
        jnp.zeros((sections, micro_tokens, model_width), BFLOAT),
        jnp.zeros((sections, micro_tokens, model_width), FLOAT),
        kept_rows,
        kept_returned,
    )
    loop_state = lax.fori_loop(0, 2 * sections - 1, forward_tick, start_state)
    saved_inputs, final_out, rows_store, returned_store = (
        loop_state[1],
        loop_state[2],
        loop_state[3],
        loop_state[4],
    )

    def attention_grads(operands):
        stream, token_mod, route_pair, upstream, is_valid, kept_pair, attn_totals, moe_totals = (
            operands
        )
        stream_grad, mod_grad, deltas = attention_backward(
            stream, token_mod, attn_weights, upstream
        )
        return (stream_grad, mod_grad, accumulate(attn_totals, deltas, is_valid), moe_totals)

    def experts_grads(operands):
        stream, token_mod, route_pair, upstream, is_valid, kept_pair, attn_totals, moe_totals = (
            operands
        )
        stream_grad, mod_grad, deltas = experts_backward(
            stream, token_mod, moe_weights, route_pair, upstream
        )
        return (stream_grad, mod_grad, attn_totals, accumulate(moe_totals, deltas, is_valid))

    def backward_tick(tick_index, loop_state):
        incoming, input_grads, attn_totals, moe_totals, ada_wgrad, ada_bgrad, table_grad = (
            loop_state
        )
        micro_index = tick_index - (sections - 1 - section_index)
        is_valid = (micro_index >= 0) & (micro_index < sections)
        clipped = jnp.clip(micro_index, 0, sections - 1)
        upstream = jnp.where(
            section_index == sections - 1, row_pick(all_cotangent, clipped), incoming
        ).astype(FLOAT)
        stream = row_pick(saved_inputs, clipped).astype(FLOAT)
        token_mod, route_pair = micro_inputs(clipped)
        kept_pair = (rows_store, returned_store)
        stream_grad, mod_grad, attn_totals, moe_totals = lax.cond(
            is_attention,
            attention_grads,
            experts_grads,
            (stream, token_mod, route_pair, upstream, is_valid, kept_pair, attn_totals, moe_totals),
        )
        image_grad = jnp.where(
            is_valid, jnp.sum(mod_grad.reshape(images_micro, PATCHES, 3 * model_width), 1), 0.0
        )
        ada_wgrad = ada_wgrad + lead_exact(row_pick(condition_rows, clipped), image_grad)
        ada_bgrad = ada_bgrad + jnp.sum(image_grad, 0)
        condition_grad = back_exact(image_grad, ada_matrix)
        embed_grad = jax.vjp(jax.nn.silu, row_pick(embedded_rows, clipped))[1](condition_grad)[0]
        table_grad = table_grad + lead_exact(row_pick(pick_blocks, clipped), embed_grad)
        input_grads = store(input_grads, stream_grad, clipped, is_valid & (section_index == 0))
        outgoing = from_behind(stream_grad.astype(BFLOAT), "section", -1)
        return (outgoing, input_grads, attn_totals, moe_totals, ada_wgrad, ada_bgrad, table_grad)

    attn_zeros = jax.tree.map(lambda template: jnp.zeros(template.shape, FLOAT), attn_weights)
    moe_zeros = jax.tree.map(lambda template: jnp.zeros(template.shape, FLOAT), moe_weights)
    start_state = (
        jnp.zeros((micro_tokens, model_width), BFLOAT),
        jnp.zeros((sections, micro_tokens, model_width), FLOAT),
        attn_zeros,
        moe_zeros,
        jnp.zeros(ada_matrix.shape, FLOAT),
        jnp.zeros(ada_offset.shape, FLOAT),
        jnp.zeros((steps_count, model_width), FLOAT),
    )
    loop_state = lax.fori_loop(0, 2 * sections - 1, backward_tick, start_state)
    input_grads, attn_totals, moe_totals, ada_wgrad, ada_bgrad, table_grad = loop_state[1:]

    def route_counts(route_pair):
        return jnp.sum(
            (
                route_pair.reshape(-1)[:, None]
                == jnp.arange(experts_total, dtype=jnp.int32)[None, :]
            ).astype(FLOAT),
            0,
        )

    local_counts = jnp.stack([route_counts(routes_one), route_counts(routes_two)])
    own_dense = (
        lax.psum(attn_totals[0].astype(jnp.bfloat16), ("dp", "expert")).astype(jnp.float32),
        lax.psum(attn_totals[1].astype(jnp.bfloat16), ("dp", "expert")).astype(jnp.float32),
        lax.psum(attn_totals[2].astype(jnp.bfloat16), ("dp", "expert")).astype(jnp.float32),
        lax.psum(attn_totals[3].astype(jnp.bfloat16), ("dp", "expert")).astype(jnp.float32),
        lax.psum(moe_totals[0].astype(jnp.bfloat16), ("dp", "expert")).astype(jnp.float32),
        lax.psum(moe_totals[1].astype(jnp.bfloat16), ("dp", "expert")).astype(jnp.float32),
        lax.psum(moe_totals[2].astype(jnp.bfloat16), ("dp", "expert")).astype(jnp.float32),
        lax.psum(moe_totals[3].astype(jnp.bfloat16), ("dp", "expert")).astype(jnp.float32),
        lax.psum(moe_totals[4].astype(jnp.bfloat16), ("dp", "expert")).astype(jnp.float32),
        lax.psum(table_grad.astype(jnp.bfloat16), ("dp", "expert")).astype(jnp.float32),
        lax.psum(local_counts.astype(jnp.bfloat16), ("dp", "expert")).astype(jnp.float32),
    )
    own_expert = (
        lax.psum(moe_totals[5].astype(jnp.bfloat16), "dp").astype(jnp.float32),
        lax.psum(moe_totals[6].astype(jnp.bfloat16), "dp").astype(jnp.float32),
        lax.psum(moe_totals[7].astype(jnp.bfloat16), "dp").astype(jnp.float32),
        lax.psum(moe_totals[8].astype(jnp.bfloat16), "dp").astype(jnp.float32),
    )
    stacked = [item[None] for item in own_dense] + [item[None] for item in own_expert]
    collected = (
        lax.all_gather(stacked[0].astype(jnp.bfloat16), "section", axis=0, tiled=True).astype(
            jnp.float32
        ),
        lax.all_gather(stacked[1].astype(jnp.bfloat16), "section", axis=0, tiled=True).astype(
            jnp.float32
        ),
        lax.all_gather(stacked[2].astype(jnp.bfloat16), "section", axis=0, tiled=True).astype(
            jnp.float32
        ),
        lax.all_gather(stacked[3].astype(jnp.bfloat16), "section", axis=0, tiled=True).astype(
            jnp.float32
        ),
        lax.all_gather(stacked[4].astype(jnp.bfloat16), "section", axis=0, tiled=True).astype(
            jnp.float32
        ),
        lax.all_gather(stacked[5].astype(jnp.bfloat16), "section", axis=0, tiled=True).astype(
            jnp.float32
        ),
        lax.all_gather(stacked[6].astype(jnp.bfloat16), "section", axis=0, tiled=True).astype(
            jnp.float32
        ),
        lax.all_gather(stacked[7].astype(jnp.bfloat16), "section", axis=0, tiled=True).astype(
            jnp.float32
        ),
        lax.all_gather(stacked[8].astype(jnp.bfloat16), "section", axis=0, tiled=True).astype(
            jnp.float32
        ),
        lax.all_gather(stacked[9].astype(jnp.bfloat16), "section", axis=0, tiled=True).astype(
            jnp.float32
        ),
        lax.all_gather(stacked[10].astype(jnp.bfloat16), "section", axis=0, tiled=True).astype(
            jnp.float32
        ),
        lax.all_gather(stacked[11].astype(jnp.bfloat16), "section", axis=0, tiled=True).astype(
            jnp.float32
        ),
        lax.all_gather(stacked[12].astype(jnp.bfloat16), "section", axis=0, tiled=True).astype(
            jnp.float32
        ),
        lax.all_gather(stacked[13].astype(jnp.bfloat16), "section", axis=0, tiled=True).astype(
            jnp.float32
        ),
        lax.all_gather(stacked[14].astype(jnp.bfloat16), "section", axis=0, tiled=True).astype(
            jnp.float32
        ),
    )
    attn_out = [collected[number][0::2] for number in range(4)]
    moe_out = [collected[number][1::2] for number in range(4, 9)]
    table_out = jnp.sum(collected[9], 0)
    counts_out = jnp.sum(collected[10], 0)
    expert_out = [collected[number][1::2] for number in range(11, 15)]
    ada_sums = (
        lax.psum(ada_wgrad[None].astype(jnp.bfloat16), ("dp", "expert")).astype(jnp.float32),
        lax.psum(ada_bgrad[None].astype(jnp.bfloat16), ("dp", "expert")).astype(jnp.float32),
    )
    output_rows, input_rows = (
        lax.psum_scatter(
            final_out.reshape(sections * micro_tokens, model_width).astype(jnp.bfloat16),
            "section",
            scatter_dimension=0,
            tiled=True,
        ).astype(jnp.float32),
        lax.psum_scatter(
            input_grads.reshape(sections * micro_tokens, model_width).astype(jnp.bfloat16),
            "section",
            scatter_dimension=0,
            tiled=True,
        ).astype(jnp.float32),
    )
    return (
        output_rows.astype(BFLOAT),
        input_rows,
        table_out,
        ada_sums[0],
        ada_sums[1],
        attn_out[0],
        attn_out[1],
        attn_out[2],
        attn_out[3],
        moe_out[0],
        moe_out[1],
        moe_out[2],
        moe_out[3],
        moe_out[4],
        expert_out[0],
        expert_out[1],
        expert_out[2],
        expert_out[3],
        counts_out.astype(jnp.int32),
    )


def solution(mesh):
    placed = (
        P(("section", "dp", "expert"), None),
        P(("section", "dp", "expert")),
        P(("section", "dp", "expert"), None),
        P(("section", "dp", "expert"), None),
        P(("section", "dp", "expert"), None),
        P(),
        P("section", None, None),
        P("section", None),
        P(),
        P(),
        P(),
        P(),
        P(),
        P(),
        P(),
        P(),
        P(),
        P(None, "expert", None, None),
        P(None, "expert", None),
        P(None, "expert", None, None),
        P(None, "expert", None),
    )
    return jax.shard_map(
        shards,
        mesh=mesh,
        in_specs=placed,
        out_specs=(
            P(("section", "dp", "expert"), None),
            P(("section", "dp", "expert"), None),
            P(),
            P("section", None, None),
            P("section", None),
            P(),
            P(),
            P(),
            P(),
            P(),
            P(),
            P(),
            P(),
            P(),
            P(None, "expert", None, None),
            P(None, "expert", None),
            P(None, "expert", None, None),
            P(None, "expert", None),
            P(),
        ),
        check_vma=False,
    )
```

profile of v0, /device:TPU:0, one launch (start us, length us, event | category | flops | bytes accessed | tf_op | source)
XLA Modules:
  0.0 2786.6 jit_solution(13650735606522188083)
XLA Ops:
  79.5 649.1 %while.68 = (s32[]{:T(128)}, bf16[256,384]{1,0:T(8,128)(2,1)S(1)}, bf16[4,256,384]{2,1,0:T(8,128)(2,1)}, bf16[4,256,384]{2,1,0:T(8,128)(2,1)}, pred[]{:T(512)}, ...) while((s32[]{:T(128)}, bf16[256,384]{1,0:T(8,128)(2,1)S(1)}, ...), condition=%wide.region_16.19_spmd, body=%wide.region_0.18_spmd.sunk | while | flops 3655931648 | bytes 39728652 | solution.py:508
  94.1 73.4 %collective-permute-start = (bf16[256,384]{1,0:T(8,128)(2,1)S(1)}, bf16[256,384]{1,0:T(8,128)(2,1)S(1)}, u32[]{:S(2)}, u32[]{:S(2)}) collective-permute-start(bf16[256,384]{1,0:T(8,128)(2,1)S(1)} %get-tuple-element.2834), channel_id=1, source_target_pairs={{0,8},{8,16},{16,24},{1,9},{9,17},{17,25},{2,10},{10,18},{18,26},{... | collective-permute-start | bytes 589832 | tf_op jit(solution)/shard_map/while/body/eval_jaxpr/ppermute | solution.py:19
  184.8 73.8 %collective-permute-start = (bf16[256,384]{1,0:T(8,128)(2,1)S(1)}, bf16[256,384]{1,0:T(8,128)(2,1)S(1)}, u32[]{:S(2)}, u32[]{:S(2)}) collective-permute-start(bf16[256,384]{1,0:T(8,128)(2,1)S(1)} %get-tuple-element.2834), channel_id=1, source_target_pairs={{0,8},{8,16},{16,24},{1,9},{9,17},{17,25},{2,10},{10,18},{18,26},{... | collective-permute-start | bytes 589832 | tf_op jit(solution)/shard_map/while/body/eval_jaxpr/ppermute | solution.py:19
  275.9 73.8 %collective-permute-start = (bf16[256,384]{1,0:T(8,128)(2,1)S(1)}, bf16[256,384]{1,0:T(8,128)(2,1)S(1)}, u32[]{:S(2)}, u32[]{:S(2)}) collective-permute-start(bf16[256,384]{1,0:T(8,128)(2,1)S(1)} %get-tuple-element.2834), channel_id=1, source_target_pairs={{0,8},{8,16},{16,24},{1,9},{9,17},{17,25},{2,10},{10,18},{18,26},{... | collective-permute-start | bytes 589832 | tf_op jit(solution)/shard_map/while/body/eval_jaxpr/ppermute | solution.py:19
  367.0 73.8 %collective-permute-start = (bf16[256,384]{1,0:T(8,128)(2,1)S(1)}, bf16[256,384]{1,0:T(8,128)(2,1)S(1)}, u32[]{:S(2)}, u32[]{:S(2)}) collective-permute-start(bf16[256,384]{1,0:T(8,128)(2,1)S(1)} %get-tuple-element.2834), channel_id=1, source_target_pairs={{0,8},{8,16},{16,24},{1,9},{9,17},{17,25},{2,10},{10,18},{18,26},{... | collective-permute-start | bytes 589832 | tf_op jit(solution)/shard_map/while/body/eval_jaxpr/ppermute | solution.py:19
  458.1 73.8 %collective-permute-start = (bf16[256,384]{1,0:T(8,128)(2,1)S(1)}, bf16[256,384]{1,0:T(8,128)(2,1)S(1)}, u32[]{:S(2)}, u32[]{:S(2)}) collective-permute-start(bf16[256,384]{1,0:T(8,128)(2,1)S(1)} %get-tuple-element.2834), channel_id=1, source_target_pairs={{0,8},{8,16},{16,24},{1,9},{9,17},{17,25},{2,10},{10,18},{18,26},{... | collective-permute-start | bytes 589832 | tf_op jit(solution)/shard_map/while/body/eval_jaxpr/ppermute | solution.py:19
  549.2 77.7 %collective-permute-start = (bf16[256,384]{1,0:T(8,128)(2,1)S(1)}, bf16[256,384]{1,0:T(8,128)(2,1)S(1)}, u32[]{:S(2)}, u32[]{:S(2)}) collective-permute-start(bf16[256,384]{1,0:T(8,128)(2,1)S(1)} %get-tuple-element.2834), channel_id=1, source_target_pairs={{0,8},{8,16},{16,24},{1,9},{9,17},{17,25},{2,10},{10,18},{18,26},{... | collective-permute-start | bytes 589832 | tf_op jit(solution)/shard_map/while/body/eval_jaxpr/ppermute | solution.py:19
  644.2 81.2 %collective-permute-start = (bf16[256,384]{1,0:T(8,128)(2,1)S(1)}, bf16[256,384]{1,0:T(8,128)(2,1)S(1)}, u32[]{:S(2)}, u32[]{:S(2)}) collective-permute-start(bf16[256,384]{1,0:T(8,128)(2,1)S(1)} %get-tuple-element.2834), channel_id=1, source_target_pairs={{0,8},{8,16},{16,24},{1,9},{9,17},{17,25},{2,10},{10,18},{18,26},{... | collective-permute-start | bytes 589832 | tf_op jit(solution)/shard_map/while/body/eval_jaxpr/ppermute | solution.py:19
  744.4 1387.2 %while.69 = (s32[]{:T(128)}, bf16[256,384]{1,0:T(8,128)(2,1)S(1)}, bf16[4,256,384]{2,1,0:T(8,128)(2,1)}, f32[384,1152]{1,0:T(8,128)}, f32[768]{0:T(1024)}, /*ind...) while((s32[]{:T(128)}, bf16[256,384]{1,0:T(8,128)(2,1)S(1)}, ...), condition=%wide.region_52.55_spmd.clone, body=%wide.region_18.54_spmd.clone.sunk | while | flops 11010491392 | bytes 309456192 | solution.py:576
  747.6 42.9 %conditional.6 = (f32[384,1152]{1,0:T(8,128)}, f32[768]{0:T(1024)}, f32[384,384]{1,0:T(8,128)}, f32[384]{0:T(512)}, f32[384,4]{0,1:T(4,128)}, /*index=5*/f32[384...) conditional(s32[]{:T(128)} %convert_element_type.716, ...), branch_computations={%region_19.41_spmd, %region_40.52_spmd} | conditional | flops 11001713664 | bytes 272932224 | solution.py:547
  803.1 133.4 %collective-permute-done.1 = bf16[256,384]{1,0:T(8,128)(2,1)S(1)} collective-permute-done((bf16[256,384]{1,0:T(8,128)(2,1)S(1)}, bf16[256,384]{1,0:T(8,128)(2,1)S(1)}, u32[]{:S(2)}, u32[]{:S(2)}) %collective-permute-start.1) | collective-permute-done | bytes 196640 | tf_op jit(solution)/shard_map/while/body/eval_jaxpr/ppermute | solution.py:19
  986.5 146.2 %collective-permute-done.1 = bf16[256,384]{1,0:T(8,128)(2,1)S(1)} collective-permute-done((bf16[256,384]{1,0:T(8,128)(2,1)S(1)}, bf16[256,384]{1,0:T(8,128)(2,1)S(1)}, u32[]{:S(2)}, u32[]{:S(2)}) %collective-permute-start.1) | collective-permute-done | bytes 196640 | tf_op jit(solution)/shard_map/while/body/eval_jaxpr/ppermute | solution.py:19
  1182.7 148.6 %collective-permute-done.1 = bf16[256,384]{1,0:T(8,128)(2,1)S(1)} collective-permute-done((bf16[256,384]{1,0:T(8,128)(2,1)S(1)}, bf16[256,384]{1,0:T(8,128)(2,1)S(1)}, u32[]{:S(2)}, u32[]{:S(2)}) %collective-permute-start.1) | collective-permute-done | bytes 196640 | tf_op jit(solution)/shard_map/while/body/eval_jaxpr/ppermute | solution.py:19
  1334.6 32.0 %conditional.6 = (f32[384,1152]{1,0:T(8,128)}, f32[768]{0:T(1024)}, f32[384,384]{1,0:T(8,128)}, f32[384]{0:T(512)}, f32[384,4]{0,1:T(4,128)}, /*index=5*/f32[384...) conditional(s32[]{:T(128)} %convert_element_type.716, ...), branch_computations={%region_19.41_spmd, %region_40.52_spmd} | conditional | flops 11001713664 | bytes 272932224 | solution.py:547
  1381.4 148.4 %collective-permute-done.1 = bf16[256,384]{1,0:T(8,128)(2,1)S(1)} collective-permute-done((bf16[256,384]{1,0:T(8,128)(2,1)S(1)}, bf16[256,384]{1,0:T(8,128)(2,1)S(1)}, u32[]{:S(2)}, u32[]{:S(2)}) %collective-permute-start.1) | collective-permute-done | bytes 196640 | tf_op jit(solution)/shard_map/while/body/eval_jaxpr/ppermute | solution.py:19
  1579.9 148.4 %collective-permute-done.1 = bf16[256,384]{1,0:T(8,128)(2,1)S(1)} collective-permute-done((bf16[256,384]{1,0:T(8,128)(2,1)S(1)}, bf16[256,384]{1,0:T(8,128)(2,1)S(1)}, u32[]{:S(2)}, u32[]{:S(2)}) %collective-permute-start.1) | collective-permute-done | bytes 196640 | tf_op jit(solution)/shard_map/while/body/eval_jaxpr/ppermute | solution.py:19
  1778.4 148.6 %collective-permute-done.1 = bf16[256,384]{1,0:T(8,128)(2,1)S(1)} collective-permute-done((bf16[256,384]{1,0:T(8,128)(2,1)S(1)}, bf16[256,384]{1,0:T(8,128)(2,1)S(1)}, u32[]{:S(2)}, u32[]{:S(2)}) %collective-permute-start.1) | collective-permute-done | bytes 196640 | tf_op jit(solution)/shard_map/while/body/eval_jaxpr/ppermute | solution.py:19
  1930.2 32.0 %conditional.6 = (f32[384,1152]{1,0:T(8,128)}, f32[768]{0:T(1024)}, f32[384,384]{1,0:T(8,128)}, f32[384]{0:T(512)}, f32[384,4]{0,1:T(4,128)}, /*index=5*/f32[384...) conditional(s32[]{:T(128)} %convert_element_type.716, ...), branch_computations={%region_19.41_spmd, %region_40.52_spmd} | conditional | flops 11001713664 | bytes 272932224 | solution.py:547
  1977.0 148.4 %collective-permute-done.1 = bf16[256,384]{1,0:T(8,128)(2,1)S(1)} collective-permute-done((bf16[256,384]{1,0:T(8,128)(2,1)S(1)}, bf16[256,384]{1,0:T(8,128)(2,1)S(1)}, u32[]{:S(2)}, u32[]{:S(2)}) %collective-permute-start.1) | collective-permute-done | bytes 196640 | tf_op jit(solution)/shard_map/while/body/eval_jaxpr/ppermute | solution.py:19
  2147.5 165.6 %all-reduce.8.cloned.1.call-done = (bf16[1,1000,384]{2,1,0:T(8,128)(2,1)}, bf16[1,384,1152]{2,1,0:T(8,128)(2,1)}, bf16[1,384,1152]{2,1,0:T(8,128)(2,1)}, bf16[1,...) async-done(((bf16[1,1000,384]{2,1,0:T(8,128)(2,1)}, bf16[1,384,1152]{2,1,0:T(8,128)(2,1)}, bf16[1,384,1152]{2,1,0:T(8,128)(2,1)}, ...) | async-done | bytes 7550992 | tf_op jit(solution)/shard_map/psum | solution.py:599
  2456.8 37.3 %all-gather.22.cloned.1.call-done = bf16[4,1,384,1536]{3,2,1,0:T(8,128)(2,1)} async-done(((bf16[1,1,384,1536]{3,2,1,0:T(8,128)(2,1)}), bf16[4,1,384,1536]{3,2,1,0:T(8,128)(2,1)}) %all-gather.22.cloned.1.call-update) | async-done | bytes 4718608 | tf_op jit(solution)/shard_map/all_gather | solution.py:643
  2498.6 54.4 %all-gather.24.cloned.1.call-done = bf16[4,1,1536,384]{3,2,1,0:T(8,128)(2,1)} async-done(((bf16[1,1,1536,384]{3,2,1,0:T(8,128)(2,1)}), bf16[4,1,1536,384]{3,2,1,0:T(8,128)(2,1)}) %all-gather.24.cloned.1.call-update) | async-done | bytes 4718608 | tf_op jit(solution)/shard_map/all_gather | solution.py:649
  2557.2 93.9 %all-gather.18.cloned.1.call-done = bf16[4,384,3072]{2,1,0:T(8,128)(2,1)} async-done(((bf16[1,384,3072]{2,1,0:T(8,128)(2,1)}), bf16[4,384,3072]{2,1,0:T(8,128)(2,1)}) %all-gather.18.cloned.1.call-update) | async-done | bytes 9437200 | tf_op jit(solution)/shard_map/all_gather | solution.py:625
  2658.5 90.6 %all-gather.20.cloned.1.call-done = bf16[4,3072,384]{2,1,0:T(8,128)(2,1)} async-done(((bf16[1,3072,384]{2,1,0:T(8,128)(2,1)}), bf16[4,3072,384]{2,1,0:T(8,128)(2,1)}) %all-gather.20.cloned.1.call-update) | async-done | bytes 9437200 | tf_op jit(solution)/shard_map/all_gather | solution.py:631
  (1278 shorter events, 941.3 us)
Async XLA Ops:
  8.1 2305.0 %all-reduce.8.cloned.1.call-start = ((), (), s32[]{:S(2)}) async-start(), calls=%async_computation.17 | async-start | bytes 15101952 | tf_op jit(solution)/shard_map/psum | solution.py:599
  184.8 77.0 %collective-permute-start = (bf16[256,384]{1,0:T(8,128)(2,1)S(1)}, bf16[256,384]{1,0:T(8,128)(2,1)S(1)}, u32[]{:S(2)}, u32[]{:S(2)}) collective-permute-start(bf16[256,384]{1,0:T(8,128)(2,1)S(1)} %get-tuple-element.2834), channel_id=1, source_target_pairs={{0,8},{8,16},{16,24},{1,9},{9,17},{17,25},{2,10},{10,18},{18,26},{... | collective-permute-start | bytes 589832 | tf_op jit(solution)/shard_map/while/body/eval_jaxpr/ppermute | solution.py:19
  275.9 77.0 %collective-permute-start = (bf16[256,384]{1,0:T(8,128)(2,1)S(1)}, bf16[256,384]{1,0:T(8,128)(2,1)S(1)}, u32[]{:S(2)}, u32[]{:S(2)}) collective-permute-start(bf16[256,384]{1,0:T(8,128)(2,1)S(1)} %get-tuple-element.2834), channel_id=1, source_target_pairs={{0,8},{8,16},{16,24},{1,9},{9,17},{17,25},{2,10},{10,18},{18,26},{... | collective-permute-start | bytes 589832 | tf_op jit(solution)/shard_map/while/body/eval_jaxpr/ppermute | solution.py:19
  367.0 77.0 %collective-permute-start = (bf16[256,384]{1,0:T(8,128)(2,1)S(1)}, bf16[256,384]{1,0:T(8,128)(2,1)S(1)}, u32[]{:S(2)}, u32[]{:S(2)}) collective-permute-start(bf16[256,384]{1,0:T(8,128)(2,1)S(1)} %get-tuple-element.2834), channel_id=1, source_target_pairs={{0,8},{8,16},{16,24},{1,9},{9,17},{17,25},{2,10},{10,18},{18,26},{... | collective-permute-start | bytes 589832 | tf_op jit(solution)/shard_map/while/body/eval_jaxpr/ppermute | solution.py:19
  458.1 77.0 %collective-permute-start = (bf16[256,384]{1,0:T(8,128)(2,1)S(1)}, bf16[256,384]{1,0:T(8,128)(2,1)S(1)}, u32[]{:S(2)}, u32[]{:S(2)}) collective-permute-start(bf16[256,384]{1,0:T(8,128)(2,1)S(1)} %get-tuple-element.2834), channel_id=1, source_target_pairs={{0,8},{8,16},{16,24},{1,9},{9,17},{17,25},{2,10},{10,18},{18,26},{... | collective-permute-start | bytes 589832 | tf_op jit(solution)/shard_map/while/body/eval_jaxpr/ppermute | solution.py:19
  549.2 80.9 %collective-permute-start = (bf16[256,384]{1,0:T(8,128)(2,1)S(1)}, bf16[256,384]{1,0:T(8,128)(2,1)S(1)}, u32[]{:S(2)}, u32[]{:S(2)}) collective-permute-start(bf16[256,384]{1,0:T(8,128)(2,1)S(1)} %get-tuple-element.2834), channel_id=1, source_target_pairs={{0,8},{8,16},{16,24},{1,9},{9,17},{17,25},{2,10},{10,18},{18,26},{... | collective-permute-start | bytes 589832 | tf_op jit(solution)/shard_map/while/body/eval_jaxpr/ppermute | solution.py:19
  644.2 84.4 %collective-permute-start = (bf16[256,384]{1,0:T(8,128)(2,1)S(1)}, bf16[256,384]{1,0:T(8,128)(2,1)S(1)}, u32[]{:S(2)}, u32[]{:S(2)}) collective-permute-start(bf16[256,384]{1,0:T(8,128)(2,1)S(1)} %get-tuple-element.2834), channel_id=1, source_target_pairs={{0,8},{8,16},{16,24},{1,9},{9,17},{17,25},{2,10},{10,18},{18,26},{... | collective-permute-start | bytes 589832 | tf_op jit(solution)/shard_map/while/body/eval_jaxpr/ppermute | solution.py:19
  792.0 144.4 %collective-permute-start.1 = (bf16[256,384]{1,0:T(8,128)(2,1)S(1)}, bf16[256,384]{1,0:T(8,128)(2,1)S(1)}, u32[]{:S(2)}, u32[]{:S(2)}) collective-permute-start(bf16[256,384]{1,0:T(8,128)(2,1)S(1)} %fusion.219), channel_id=1, source_target_pairs={{8,0},{16,8},{24,16},{9,1},{17,9},{25,17},{10,2},{18,10},{26,18},{... | collective-permute-start | bytes 589832 | tf_op jit(solution)/shard_map/while/body/eval_jaxpr/ppermute | solution.py:19
  973.2 159.5 %collective-permute-start.1 = (bf16[256,384]{1,0:T(8,128)(2,1)S(1)}, bf16[256,384]{1,0:T(8,128)(2,1)S(1)}, u32[]{:S(2)}, u32[]{:S(2)}) collective-permute-start(bf16[256,384]{1,0:T(8,128)(2,1)S(1)} %fusion.219), channel_id=1, source_target_pairs={{8,0},{16,8},{24,16},{9,1},{17,9},{25,17},{10,2},{18,10},{26,18},{... | collective-permute-start | bytes 589832 | tf_op jit(solution)/shard_map/while/body/eval_jaxpr/ppermute | solution.py:19
  1169.4 161.9 %collective-permute-start.1 = (bf16[256,384]{1,0:T(8,128)(2,1)S(1)}, bf16[256,384]{1,0:T(8,128)(2,1)S(1)}, u32[]{:S(2)}, u32[]{:S(2)}) collective-permute-start(bf16[256,384]{1,0:T(8,128)(2,1)S(1)} %fusion.219), channel_id=1, source_target_pairs={{8,0},{16,8},{24,16},{9,1},{17,9},{25,17},{10,2},{18,10},{26,18},{... | collective-permute-start | bytes 589832 | tf_op jit(solution)/shard_map/while/body/eval_jaxpr/ppermute | solution.py:19
  1368.1 161.8 %collective-permute-start.1 = (bf16[256,384]{1,0:T(8,128)(2,1)S(1)}, bf16[256,384]{1,0:T(8,128)(2,1)S(1)}, u32[]{:S(2)}, u32[]{:S(2)}) collective-permute-start(bf16[256,384]{1,0:T(8,128)(2,1)S(1)} %fusion.219), channel_id=1, source_target_pairs={{8,0},{16,8},{24,16},{9,1},{17,9},{25,17},{10,2},{18,10},{26,18},{... | collective-permute-start | bytes 589832 | tf_op jit(solution)/shard_map/while/body/eval_jaxpr/ppermute | solution.py:19
  1566.6 161.7 %collective-permute-start.1 = (bf16[256,384]{1,0:T(8,128)(2,1)S(1)}, bf16[256,384]{1,0:T(8,128)(2,1)S(1)}, u32[]{:S(2)}, u32[]{:S(2)}) collective-permute-start(bf16[256,384]{1,0:T(8,128)(2,1)S(1)} %fusion.219), channel_id=1, source_target_pairs={{8,0},{16,8},{24,16},{9,1},{17,9},{25,17},{10,2},{18,10},{26,18},{... | collective-permute-start | bytes 589832 | tf_op jit(solution)/shard_map/while/body/eval_jaxpr/ppermute | solution.py:19
  1765.0 161.9 %collective-permute-start.1 = (bf16[256,384]{1,0:T(8,128)(2,1)S(1)}, bf16[256,384]{1,0:T(8,128)(2,1)S(1)}, u32[]{:S(2)}, u32[]{:S(2)}) collective-permute-start(bf16[256,384]{1,0:T(8,128)(2,1)S(1)} %fusion.219), channel_id=1, source_target_pairs={{8,0},{16,8},{24,16},{9,1},{17,9},{25,17},{10,2},{18,10},{26,18},{... | collective-permute-start | bytes 589832 | tf_op jit(solution)/shard_map/while/body/eval_jaxpr/ppermute | solution.py:19
  1963.7 161.8 %collective-permute-start.1 = (bf16[256,384]{1,0:T(8,128)(2,1)S(1)}, bf16[256,384]{1,0:T(8,128)(2,1)S(1)}, u32[]{:S(2)}, u32[]{:S(2)}) collective-permute-start(bf16[256,384]{1,0:T(8,128)(2,1)S(1)} %fusion.219), channel_id=1, source_target_pairs={{8,0},{16,8},{24,16},{9,1},{17,9},{25,17},{10,2},{18,10},{26,18},{... | collective-permute-start | bytes 589832 | tf_op jit(solution)/shard_map/while/body/eval_jaxpr/ppermute | solution.py:19
  2142.9 194.7 %all-reduce.10.cloned.1.call-start = ((), (), s32[]{:S(2)}) async-start(), calls=%async_computation.18 | async-start | bytes 4718592 | tf_op jit(solution)/shard_map/psum | solution.py:603
  2146.9 297.6 %reduce-scatter.5.cloned.1.call-start = ((), (), s32[]{:S(2)}) async-start(), calls=%async_computation.9 | async-start | bytes 983040 | tf_op jit(solution)/shard_map/reduce_scatter | solution.py:672
  2147.4 300.1 %all-gather.16.cloned.1.call-start = ((), (), s32[]{:S(2)}) async-start(), calls=%async_computation.12 | async-start | bytes 1474560 | tf_op jit(solution)/shard_map/all_gather | solution.py:616
  2313.1 136.6 %all-gather.12.cloned.1.call-start = ((), (), s32[]{:S(2)}) async-start(), calls=%async_computation.10 | async-start | bytes 3840000 | tf_op jit(solution)/shard_map/all_gather | solution.py:637
  2313.6 139.6 %all-gather.14.cloned.1.call-start = ((), (), s32[]{:S(2)}) async-start(), calls=%async_computation.11 | async-start | bytes 4423680 | tf_op jit(solution)/shard_map/all_gather | solution.py:610
  2314.4 179.7 %all-gather.22.cloned.1.call-start = ((), (), s32[]{:S(2)}) async-start(), calls=%async_computation.15 | async-start | bytes 5898240 | tf_op jit(solution)/shard_map/all_gather | solution.py:643
  2337.6 215.4 %all-gather.24.cloned.1.call-start = ((), (), s32[]{:S(2)}) async-start(), calls=%async_computation.16 | async-start | bytes 5898240 | tf_op jit(solution)/shard_map/all_gather | solution.py:649
  2338.3 312.7 %all-gather.18.cloned.1.call-start = ((), (), s32[]{:S(2)}) async-start(), calls=%async_computation.13 | async-start | bytes 11796480 | tf_op jit(solution)/shard_map/all_gather | solution.py:625
  2338.9 410.2 %all-gather.20.cloned.1.call-start = ((), (), s32[]{:S(2)}) async-start(), calls=%async_computation.14 | async-start | bytes 11796480 | tf_op jit(solution)/shard_map/all_gather | solution.py:631
  2339.5 439.2 %reduce-scatter.3.cloned.1.call-start = ((), (), s32[]{:S(2)}) async-start(), calls=%async_computation.8 | async-start | bytes 983040 | tf_op jit(solution)/shard_map/reduce_scatter | solution.py:666
  (290 other events, 6576.3 us)
Sparse Core Ops, SparseCore 0:
  2143.0 169.9 all-reduce.7
  2316.0 21.5 all-reduce.9
Sparse Core Ops, SparseCore 1:
  2150.2 33.6 reduce-scatter.4
  2313.2 27.4 all-gather.15
  2342.3 43.3 all-gather.11
  2387.5 47.5 all-gather.13
  2437.1 56.9 all-gather.21
  2496.1 56.9 all-gather.23
  2554.9 96.1 all-gather.17
  2652.9 96.1 all-gather.19
  2752.7 26.0 reduce-scatter.2
where the time goes:
time: 2810 us; the launch traced here: 2790 us
  waiting for transfers between devices  1520 us (54%)
  starting transfers between devices  537 us (19%)
  local copies, waits for them, and re-layouts  205 us (7%)
  other arithmetic  195 us (7%)
  matrix products  148 us (5%)
  blocking collectives  142 us (5%)
    ppermute x14, waiting for transfers between devices, from_behind(): return lax.ppermute(x, axis, pairs)  1030 us
    ppermute x14, starting transfers between devices, from_behind(): return lax.ppermute(x, axis, pairs)  537 us
    psum x1, waiting for transfers between devices, shards(): lax.psum(table_grad.astype(jnp.bfloat16), ('dp', 'expert'))  166 us
    all_gather x1, waiting for transfers between devices, shards(): lax.all_gather(stacked[5].astype(jnp.bfloat16), 'section', axis=0, tiled=...  93.9 us
    all_gather x1, waiting for transfers between devices, shards(): lax.all_gather(stacked[7].astype(jnp.bfloat16), 'section', axis=0, tiled=...  90.6 us
  transfers between devices with their start and end apart: 25, of which 21 were waited for; matrix products, arithmetic and copies ran while one was open for 5% of the time, Pallas kernels for 0%

commit v1 on v0

v1 whole, which is shorter than its diff:
```python
import jax
import jax.numpy as jnp
from jax import lax
from jax.sharding import PartitionSpec as P

HEADS = 6
HD = 64

BFLOAT = jnp.bfloat16
FLOAT = jnp.float32
ALL = ("section", "dp", "expert")


def product(left_arg, right_arg):
    return jnp.dot(left_arg, right_arg, preferred_element_type=FLOAT)


def lead_product(left_arg, right_arg):
    return lax.dot_general(
        left_arg, right_arg, (((0,), (0,)), ((), ())), preferred_element_type=FLOAT
    )


def back_product(left_arg, right_arg):
    return lax.dot_general(
        left_arg, right_arg, (((1,), (1,)), ((), ())), preferred_element_type=FLOAT
    )


def gelu_parts(pre):
    inner = 0.7978845608028654 * (pre + 0.044715 * pre * pre * pre)
    tanh = jnp.tanh(inner)
    act = 0.5 * pre * (1.0 + tanh)
    slope = 0.5 * (1.0 + tanh) + 0.5 * pre * (1.0 - tanh * tanh) * 0.7978845608028654 * (
        1.0 + 3 * 0.044715 * pre * pre
    )
    return act, slope


def normalized(stream):
    row_mean = jnp.mean(stream, -1, keepdims=True)
    centred = stream - row_mean
    variance = jnp.mean(centred * centred, -1, keepdims=True)
    inverse = lax.rsqrt(variance + 1e-06)
    return centred * inverse, inverse


def modulate(stream, mod):
    unit, _ = normalized(stream)
    return (unit * (1.0 + mod[1]) + mod[0]).astype(BFLOAT)


def norm_backward(stream, mod, hidden_grad):
    unit, inverse = normalized(stream)
    shift_grad = jnp.sum(hidden_grad, 0)
    scale_grad = jnp.sum(hidden_grad * unit, 0)
    unit_grad = hidden_grad * (1.0 + mod[1])
    stream_grad = inverse * (
        unit_grad
        - jnp.mean(unit_grad, -1, keepdims=True)
        - unit * jnp.mean(unit_grad * unit, -1, keepdims=True)
    )
    return stream_grad, shift_grad, scale_grad


def heads_view(rows):
    return rows.astype(BFLOAT).reshape(-1, HEADS, HD)


def attention_forward(hidden, weights):
    qkv_matrix, qv_offset, out_matrix, out_offset = weights
    width = hidden.shape[1]
    projected = product(hidden, qkv_matrix)
    query = heads_view(projected[:, :width] + qv_offset[:width])
    key = heads_view(projected[:, width : 2 * width])
    value = heads_view(projected[:, 2 * width :] + qv_offset[width:])
    scores = jnp.einsum("qhd,khd->hqk", query, key, preferred_element_type=FLOAT) * HD ** (-0.5)
    probs = jax.nn.softmax(scores, -1)
    probs_low = probs.astype(BFLOAT)
    attended = (
        jnp.einsum("hqk,khd->qhd", probs_low, value, preferred_element_type=FLOAT)
        .reshape(-1, width)
        .astype(BFLOAT)
    )
    branch = product(attended, out_matrix) + out_offset
    return branch, (query, key, value, probs, probs_low, attended)


def attention_backward(hidden, weights, saved, branch_grad):
    qkv_matrix, _, out_matrix, _ = weights
    query, key, value, probs, probs_low, attended = saved
    width = hidden.shape[1]
    factor = HD ** (-0.5)
    low_grad = branch_grad.astype(BFLOAT)
    out_grad = lead_product(attended, low_grad)
    out_offset_grad = jnp.sum(low_grad.astype(FLOAT), 0)
    attended_grad = heads_view(back_product(low_grad, out_matrix))
    value_grad = jnp.einsum("hqk,qhd->khd", probs_low, attended_grad, preferred_element_type=FLOAT)
    prob_grad = jnp.einsum("qhd,khd->hqk", attended_grad, value, preferred_element_type=FLOAT)
    score_grad = (probs * (prob_grad - jnp.sum(prob_grad * probs, -1, keepdims=True))).astype(
        BFLOAT
    )
    query_grad = (
        jnp.einsum("hqk,khd->qhd", score_grad, key, preferred_element_type=FLOAT) * factor
    )
    key_grad = (
        jnp.einsum("hqk,qhd->khd", score_grad, query, preferred_element_type=FLOAT) * factor
    )
    proj_grad = jnp.concatenate(
        [item.reshape(-1, width) for item in (query_grad, key_grad, value_grad)], -1
    ).astype(BFLOAT)
    qkv_grad = lead_product(hidden, proj_grad)
    sums = jnp.sum(proj_grad.astype(FLOAT), 0)
    offset_grad = jnp.concatenate([sums[:width], sums[2 * width :]])
    hidden_grad = back_product(proj_grad, qkv_matrix)
    return hidden_grad, (qkv_grad, offset_grad, out_grad, out_offset_grad)


def expert_gates(rows, router, route_pair):
    logits = product(rows, router)
    marks = (
        route_pair[:, :, None] == jnp.arange(router.shape[1], dtype=jnp.int32)[None, None, :]
    ).any(1)
    top = jnp.max(jnp.where(marks, logits, -jnp.inf), -1, keepdims=True)
    raised = jnp.where(marks, jnp.exp(logits - top), 0.0)
    return raised / jnp.sum(raised, -1, keepdims=True)


def pick_column(table, column):
    return lax.dynamic_slice_in_dim(table, column, 1, axis=1)


def moe_forward(hidden, route_pair, weights):
    router, s_up, s_upb, s_down, s_downb, e_up, e_upb, e_down, e_downb = weights
    mine = lax.axis_index("expert")
    rows = lax.all_gather(hidden, "expert", axis=0, tiled=True)
    routes = lax.all_gather(route_pair, "expert", axis=0, tiled=True)
    gates = expert_gates(rows, router, routes)
    gate = pick_column(gates, mine)
    shared_pre = product(hidden, s_up) + s_upb
    shared_act, shared_slope = gelu_parts(shared_pre)
    shared_act = shared_act.astype(BFLOAT)
    shared_out = product(shared_act, s_down) + s_downb
    pre = product(rows, e_up[0]) + e_upb[0]
    act, slope = gelu_parts(pre)
    act = act.astype(BFLOAT)
    result = (product(act, e_down[0]) + e_downb[0]).astype(BFLOAT)
    routed = lax.psum_scatter(
        (gate * result.astype(FLOAT)).astype(BFLOAT), "expert", scatter_dimension=0, tiled=True
    )
    branch = shared_out + routed.astype(FLOAT)
    saved = (rows, routes, gates, gate, shared_act, shared_slope, act, slope, result)
    return branch, saved


def moe_backward(hidden, weights, saved, branch_grad):
    router, s_up, s_upb, s_down, s_downb, e_up, e_upb, e_down, e_downb = weights
    rows, routes, gates, gate, shared_act, shared_slope, act, slope, result = saved
    mine = lax.axis_index("expert")
    devices = lax.axis_size("expert")
    tokens_here = hidden.shape[0]
    low_grad = branch_grad.astype(BFLOAT)
    s_down_grad = lead_product(shared_act, low_grad)
    s_downb_grad = jnp.sum(low_grad.astype(FLOAT), 0)
    shared_dpre = (back_product(low_grad, s_down) * shared_slope).astype(BFLOAT)
    s_up_grad = lead_product(hidden, shared_dpre)
    s_upb_grad = jnp.sum(shared_dpre.astype(FLOAT), 0)
    hidden_grad = back_product(shared_dpre, s_up)
    row_grad = lax.all_gather(low_grad, "expert", axis=0, tiled=True).astype(FLOAT)
    gate_grad = jnp.sum(row_grad * result.astype(FLOAT), -1)
    gate_grads = lax.all_to_all(
        gate_grad.reshape(devices, tokens_here).astype(BFLOAT), "expert", 0, 0, tiled=True
    ).astype(FLOAT)
    own_gates = lax.dynamic_slice_in_dim(gates, mine * tokens_here, tokens_here, axis=0)
    gate_grads = gate_grads.T
    logit_grad = own_gates * (gate_grads - jnp.sum(own_gates * gate_grads, -1, keepdims=True))
    router_grad = lax.dot_general(
        hidden.astype(FLOAT),
        logit_grad,
        (((0,), (0,)), ((), ())),
        precision=lax.Precision.HIGHEST,
        preferred_element_type=FLOAT,
    )
    result_grad = (gate * row_grad).astype(BFLOAT)
    e_down_grad = lead_product(act, result_grad)
    e_downb_grad = jnp.sum(result_grad.astype(FLOAT), 0)
    dpre = (back_product(result_grad, e_down[0]) * slope).astype(BFLOAT)
    e_up_grad = lead_product(rows, dpre)
    e_upb_grad = jnp.sum(dpre.astype(FLOAT), 0)
    back_rows = lax.psum_scatter(
        back_product(dpre, e_up[0]).astype(BFLOAT), "expert", scatter_dimension=0, tiled=True
    )
    hidden_grad = hidden_grad + back_product(logit_grad, router.astype(FLOAT)) + back_rows
    return hidden_grad, (
        router_grad,
        s_up_grad,
        s_upb_grad,
        s_down_grad,
        s_downb_grad,
        e_up_grad,
        e_upb_grad,
        e_down_grad,
        e_downb_grad,
    )


def shards(
    tokens,
    timesteps,
    routes_one,
    routes_two,
    cotangent,
    time_table,
    ada_weight,
    ada_bias,
    qkv_weight,
    qv_bias,
    out_weight,
    out_bias,
    router_weight,
    shared_up,
    shared_up_bias,
    shared_down,
    shared_down_bias,
    expert_up,
    expert_up_bias,
    expert_down,
    expert_down_bias,
):
    width = tokens.shape[1]
    steps_count = time_table.shape[0]
    experts_total = router_weight.shape[2]
    route_sets = (routes_one, routes_two)
    steps = lax.all_gather(timesteps, "section", axis=0, tiled=True)
    embedded = jnp.take(time_table, steps, axis=0).astype(FLOAT)
    condition = jax.nn.silu(embedded).astype(BFLOAT)
    section_mod = product(condition, ada_weight[0]) + ada_bias[0].astype(FLOAT)
    mods = lax.all_to_all(section_mod, "section", 0, 0, tiled=True).reshape(-1, 3, width)

    def attn_weights(layer):
        return (
            qkv_weight[layer],
            qv_bias[layer].astype(FLOAT),
            out_weight[layer],
            out_bias[layer].astype(FLOAT),
        )

    def moe_weights(layer):
        return (
            router_weight[layer],
            shared_up[layer],
            shared_up_bias[layer].astype(FLOAT),
            shared_down[layer],
            shared_down_bias[layer].astype(FLOAT),
            expert_up[layer],
            expert_up_bias[layer].astype(FLOAT),
            expert_down[layer],
            expert_down_bias[layer].astype(FLOAT),
        )

    streams, hiddens, branches, kept = [], [], [], []
    stream = tokens
    for block in range(4):
        layer = block // 2
        streams.append(stream)
        wide = stream.astype(FLOAT)
        hidden = modulate(wide, mods[block])
        if block % 2 == 0:
            branch, saved = attention_forward(hidden, attn_weights(layer))
        else:
            branch, saved = moe_forward(hidden, route_sets[layer], moe_weights(layer))
        hiddens.append(hidden)
        branches.append(branch)
        kept.append(saved)
        stream = (wide + mods[block][2] * branch).astype(BFLOAT)
    output = stream

    upstream = cotangent
    mod_grads = [None] * 4
    attn_grads = [None] * 2
    moe_grads = [None] * 2
    for block in (3, 2, 1, 0):
        layer = block // 2
        wide_grad = upstream.astype(FLOAT)
        gating_grad = jnp.sum(wide_grad * branches[block], 0)
        branch_grad = mods[block][2] * wide_grad
        if block % 2 == 0:
            hidden_grad, attn_grads[layer] = attention_backward(
                hiddens[block], attn_weights(layer), kept[block], branch_grad
            )
        else:
            hidden_grad, moe_grads[layer] = moe_backward(
                hiddens[block], moe_weights(layer), kept[block], branch_grad
            )
        stream_grad, shift_grad, scale_grad = norm_backward(
            streams[block].astype(FLOAT), mods[block], hidden_grad
        )
        mod_grads[block] = jnp.concatenate([shift_grad, scale_grad, gating_grad])
        token_grad = wide_grad + stream_grad
        upstream = token_grad.astype(BFLOAT)

    section_grads = lax.all_to_all(jnp.stack(mod_grads), "section", 0, 0, tiled=True)
    ada_part = lead_product(condition, section_grads.astype(BFLOAT))
    condition_grad = back_product(section_grads, ada_weight[0].astype(FLOAT))
    condition_grad = lax.psum(condition_grad, "section")
    embed_grad = jax.vjp(jax.nn.silu, embedded)[1](condition_grad)[0]
    marks = (steps[:, None] == jnp.arange(steps_count, dtype=jnp.int32)[None, :]).astype(FLOAT)
    table_part = lead_product(marks, embed_grad)

    def counted(route_pair):
        return jnp.sum(
            (
                route_pair.reshape(-1)[:, None]
                == jnp.arange(experts_total, dtype=jnp.int32)[None, :]
            ).astype(jnp.int32),
            0,
        )

    def total(parts, axes):
        return lax.psum(parts.astype(BFLOAT), axes).astype(FLOAT)

    both_attn = [jnp.stack([attn_grads[0][n], attn_grads[1][n]]) for n in range(4)]
    both_moe = [jnp.stack([moe_grads[0][n], moe_grads[1][n]]) for n in range(9)]
    counts = lax.psum(jnp.stack([counted(routes_one), counted(routes_two)]), ALL)
    attn_out = [total(item, ALL) for item in both_attn]
    moe_out = [total(item, ALL) for item in both_moe[:5]]
    expert_out = [total(item, ("section", "dp"))[:, None] for item in both_moe[5:]]
    table_out = total(table_part, ("dp", "expert"))
    ada_out = total(ada_part, ("dp", "expert"))[None]
    ada_bias_out = total(jnp.sum(section_grads, 0), ("dp", "expert"))[None]
    return (
        output,
        token_grad,
        table_out,
        ada_out,
        ada_bias_out,
        *attn_out,
        *moe_out,
        *expert_out,
        counts,
    )


def solution(mesh):
    rows = P(ALL, None)
    whole = P()
    placed = (
        rows,
        P(ALL),
        rows,
        rows,
        rows,
        whole,
        P("section", None, None),
        P("section", None),
        *([whole] * 9),
        P(None, "expert", None, None),
        P(None, "expert", None),
        P(None, "expert", None, None),
        P(None, "expert", None),
    )
    return jax.shard_map(
        shards,
        mesh=mesh,
        in_specs=placed,
        out_specs=(
            rows,
            rows,
            whole,
            P("section", None, None),
            P("section", None),
            *([whole] * 9),
            P(None, "expert", None, None),
            P(None, "expert", None),
            P(None, "expert", None, None),
            P(None, "expert", None),
            whole,
        ),
        check_vma=False,
    )
```

time: 2810 us -> 721 us (0.26)
  waiting for transfers between devices: 1520 us -> 233 us
  starting transfers between devices: 537 us -> 14.2 us
  local copies, waits for them, and re-layouts: 205 us -> 27.7 us
  other arithmetic: 195 us -> 65.1 us
  blocking collectives: 142 us -> 234 us
    ppermute x14 -> x0, waiting for transfers between devices: 1030 us -> none  [from_behind(): return lax.ppermute(x, axis, pairs)]
    ppermute x14 -> x0, starting transfers between devices: 537 us -> none  [from_behind(): return lax.ppermute(x, axis, pairs)]
    all_gather x7 -> x0, waiting for transfers between devices: 276 us -> none  [the longest x1 93.9 us: shards(): lax.all_gather(stacked[5].astype(jnp.bfloat16), 'section', axis=0, tiled=...]
    psum x2 -> x5, blocking collectives: 31.9 us -> 126 us  [the longest x3 78.5 us: total(): return lax.psum(parts.astype(BFLOAT), axes).astype(FLOAT)]
    cond x350 -> x0, local copies, waits for them, and re-layouts: 54.8 us -> none
    dynamic_slice x56 -> x2, local copies, waits for them, and re-layouts: 49.9 us -> 0.02 us  [pick_column(): return lax.dynamic_slice_in_dim(table, column, 1, axis=1)]
    dot_general x79 -> x27, matrix products: 89.6 us -> 47.6 us  [the longest x15 39.6 us: product(): return jnp.dot(left_arg, right_arg, preferred_element_type=FLOAT)]
    slice x20 -> x3, other arithmetic: 42.1 us -> 0.86 us  [shards(): stream = (wide + mods[block][2] * branch).astype(BFLOAT)]
  transfers between devices with their start and end apart: 25 -> 11, of which waited for: 21 -> 4; matrix products, arithmetic and copies ran while one was open for 5% -> 15% of each run, Pallas kernels for 0% -> 0%
where the time goes in v1:
time: 721 us; the launch traced here: 714 us
  blocking collectives  234 us (32%)
  waiting for transfers between devices  233 us (32%)
  matrix products  123 us (17%)
  other arithmetic  65.1 us (9%)
  local copies, waits for them, and re-layouts  27.7 us (4%)
  between operations  17 us (2%)
  starting transfers between devices  14.2 us (2%)
    psum x3, waiting for transfers between devices, total(): return lax.psum(parts.astype(BFLOAT), axes).astype(FLOAT)  208 us
    psum x3, blocking collectives, total(): return lax.psum(parts.astype(BFLOAT), axes).astype(FLOAT)  78.5 us
    dot_general x15, matrix products, back_product(): lax.dot_general(left_arg, right_arg, (((1,), (1,)), ((), ())), preferred_...  42.5 us
    dot_general x15, matrix products, product(): return jnp.dot(left_arg, right_arg, preferred_element_type=FLOAT)  39.6 us
    all_gather x2, blocking collectives, moe_backward(): lax.all_gather(low_grad, 'expert', axis=0, tiled=True).astype(FLOAT)  39.4 us
    psum x1, blocking collectives, shards(): lax.psum(jnp.stack([counted(routes_one), counted(routes_two)]), ALL)  38.3 us
    all_gather x2, blocking collectives, moe_forward(): rows = lax.all_gather(hidden, 'expert', axis=0, tiled=True)  35 us
    dot_general x14, matrix products, lead_product(): lax.dot_general(left_arg, right_arg, (((0,), (0,)), ((), ())), preferred_...  30.2 us
  transfers between devices with their start and end apart: 11, of which 4 were waited for; matrix products, arithmetic and copies ran while one was open for 15% of the time, Pallas kernels for 0%

profile of v1, /device:TPU:0, one launch (start us, length us, event | category | flops | bytes accessed | tf_op | source)
XLA Modules:
  0.0 713.7 jit_solution(3670799782260023642)
XLA Ops:
  9.9 8.8 %all-reduce = s32[4]{0:T(128)S(1)} all-reduce(s32[4]{0:T(128)S(1)} %dynamic-update-slice), channel_id=1, replica_groups=mesh['section'=4,'dp'=2,'expert'=4] {'section'}, use_global_device_ids=true, to_apply=%add | all-reduce | flops 4 | bytes 32
  29.9 12.2 %all_gather.22 = s32[1024,2]{0,1:T(2,128)S(1)} all-gather(s32[256,2]{0,1:T(2,128)} %param.23), channel_id=1, replica_groups=mesh['section'=4,'dp'=2,'expert'=4] {'expert'}, dimensions={0}, use_global_device_ids=true | all-gather | bytes 10240 | tf_op jit(solution)/shard_map/all_gather | solution.py:137
  44.3 12.0 %all_gather.24 = s32[1024,2]{0,1:T(2,128)S(1)} all-gather(s32[256,2]{0,1:T(2,128)} %param.24), channel_id=1, replica_groups=mesh['section'=4,'dp'=2,'expert'=4] {'expert'}, dimensions={0}, use_global_device_ids=true | all-gather | bytes 10240 | tf_op jit(solution)/shard_map/all_gather | solution.py:137
  64.0 15.6 %all_gather.23 = bf16[1024,384]{1,0:T(8,128)(2,1)S(1)} all-gather(bf16[256,384]{1,0:T(8,128)(2,1)S(1)} %fusion.174), channel_id=1, replica_groups=mesh['section'=4,'dp'=2,'expert'=4] {'expert'}, dimensions={0}, use_global_device_ids=true | all-gather | bytes 983040 | tf_op jit(solution)/shard_map/all_gather | solution.py:136
  88.3 21.5 %all_gather.26 = bf16[1024,384]{1,0:T(8,128)(2,1)S(1)} all-gather(bf16[256,384]{1,0:T(8,128)(2,1)S(1)} %get-tuple-element.173), channel_id=1, replica_groups=mesh['section'=4,'dp'=2,'expert'=4] {'expert'}, dimensions={0}, use_global_device_ids=true | all-gather | bytes 983040 | tf_op jit(solution)/shard_map/all_gather | solution.py:169
  109.8 4.6 convolution_add_fusion.1
  114.4 4.7 convert_reduce_fusion.1
  126.2 19.5 %all_gather.25 = bf16[1024,384]{1,0:T(8,128)(2,1)S(1)} all-gather(bf16[256,384]{1,0:T(8,128)(2,1)S(1)} %fusion.160), channel_id=1, replica_groups=mesh['section'=4,'dp'=2,'expert'=4] {'expert'}, dimensions={0}, use_global_device_ids=true | all-gather | bytes 983040 | tf_op jit(solution)/shard_map/all_gather | solution.py:136
  150.1 6.2 fusion.310
  160.7 4.9 fusion.64
  182.9 5.6 fusion.308
  195.6 13.6 %reduce-scatter.7.cloned.1.call-done = bf16[256,384]{1,0:T(8,128)(2,1)} async-done(((bf16[1024,384]{1,0:T(8,128)(2,1)}), bf16[256,384]{1,0:T(8,128)(2,1)}) %reduce-scatter.7.cloned.1.call-update) | async-done | bytes 196624 | tf_op jit(solution)/shard_map/reduce_scatter | solution.py:148
  209.2 5.6 fusion.193
  226.4 18.0 %all_gather.27 = bf16[1024,384]{1,0:T(8,128)(2,1)S(1)} all-gather(bf16[256,384]{1,0:T(8,128)(2,1)S(1)} %get-tuple-element.170), channel_id=1, replica_groups=mesh['section'=4,'dp'=2,'expert'=4] {'expert'}, dimensions={0}, use_global_device_ids=true | all-gather | bytes 983040 | tf_op jit(solution)/shard_map/all_gather | solution.py:169
  244.4 6.8 fusion.309
  254.2 6.2 fusion.311
  293.9 8.2 %reduce-scatter.11.cloned.1.call-done = bf16[256,384]{1,0:T(8,128)(2,1)} async-done(((bf16[1024,384]{1,0:T(8,128)(2,1)}), bf16[256,384]{1,0:T(8,128)(2,1)}) %reduce-scatter.11.cloned.1.call-update) | async-done | bytes 196624 | tf_op jit(solution)/shard_map/reduce_scatter | solution.py:190
  322.4 9.2 %psum.126 = f32[4,384]{1,0:T(4,128)S(1)} all-reduce(f32[4,384]{1,0:T(4,128)S(1)} %fusion.128), channel_id=1, replica_groups=mesh['section'=4,'dp'=2,'expert'=4] {'section'}, use_global_device_ids=true, to_apply=%region_48.49 | all-reduce | flops 1536 | bytes 12288 | tf_op jit(solution)/shard_map/psum | solution.py:305
  345.6 38.3 %psum.143 = s32[2,4]{1,0:T(2,128)} all-reduce(s32[2,4]{1,0:T(2,128)S(1)} %pad_add_fusion), channel_id=1, replica_groups=mesh['section'=4,'dp'=2,'expert'=4] {'section','dp','expert'}, use_global_device_ids=true, to_apply=%region_80.81 | all-reduce | flops 8 | bytes 64 | tf_op jit(solution)/shard_map/psum | solution.py:324
  386.2 23.4 %all-reduce.4 = (bf16[2,1,1536]{2,1,0:T(2,128)(2,1)S(1)}, bf16[2,1,384]{2,1,0:T(2,128)(2,1)S(1)}) all-reduce(bf16[2,1,1536]{2,1,0:T(2,128)(2,1)S(1)} %broadcast_in_dim.62, bf16[2,1,384]{2,1,0:T(2,128)(2,1)S(1)} %broadcast_in_dim.66), channel_id=1, replica_groups=mesh['section'=4,'dp'=2,'expert'=4] {'section','dp'}, use_global_device_ids=true, to_apply=%region_73.74 | all-reduce | flops 3840 | bytes 15360 | tf_op jit(solution)/shard_map/psum | solution.py:320
  414.4 40.3 %all-reduce.1 = (bf16[2,768]{1,0:T(2,128)(2,1)S(1)}, bf16[2,384]{1,0:T(2,128)(2,1)S(1)}, bf16[2,384,4]{1,2,0:T(4,128)(2,1)S(1)}, bf16[2,3072]{1,0:T(2,128)(2,1)S(1)}, bf16[2,384]{1,0:T(2,128)(2,1)S(1)}) all-reduce(bf16[2,768]{1,0:T(2,128)(2,1)S(1)} %pad_maximum_fusion.14,, ...), channel_id=1, replica_groups=mesh['section'=4,'dp'=2,'expert'=4] {'section','dp','expert'}, use_global_device_ids=true, to_apply=%region_56.57 | all-reduce | flops 12288 | bytes 49152 | tf_op jit(solution)/shard_map/psum | solution.py:320
  457.7 14.8 %psum.129 = bf16[1,1152]{1,0:T(2,128)(2,1)S(1)} all-reduce(bf16[1,1152]{1,0:T(2,128)(2,1)S(1)} %broadcast_in_dim.58), channel_id=1, replica_groups=mesh['section'=4,'dp'=2,'expert'=4] {'dp','expert'}, use_global_device_ids=true, to_apply=%region_52.53 | all-reduce | flops 1152 | bytes 4608 | tf_op jit(solution)/shard_map/psum | solution.py:320
  484.0 207.6 %all-reduce.10.cloned.1.call-done = (bf16[2,384,1152]{2,1,0:T(8,128)(2,1)}, bf16[2,384,384]{2,1,0:T(8,128)(2,1)}, bf16[2,384,3072]{2,1,0:T(8,128)(2,1)}, bf16[2,3072,384]{2,1,0:T(8,128)(2,1)}) async-done(((bf16[2,384,1152]{2,1,0:T(8,128)(2,1)}, bf16[2,384,384]{2,1,0:T(8,128)(2,1)}, bf16[2,384,3072]{2,1,0:T(8,128)(2,1)}, bf16[2,3072,384]{2,1,0:T(8,128)(2,1)}), (bf16[2,384,1152]{2,1,0:T(8,128)(2,1)}, ...) | async-done | bytes 11796496 | tf_op jit(solution)/shard_map/psum | solution.py:320
  691.6 7.5 %convert_element_type.513 = f32[2,384,3072]{2,1,0:T(8,128)} convert(bf16[2,384,3072]{2,1,0:T(8,128)(2,1)} %get-tuple-element.161) | non-fusion elementwise | flops 2359296 | bytes 14155776 | tf_op jit(solution)/shard_map/convert_element_type | solution.py:320
  (496 shorter events, 181.5 us)
Async XLA Ops:
  22.7 33.6 %all-to-all-start = ((f32[4,1,1152]{2,1,0:T(1,128)}), f32[4,1,1152]{2,1,0:T(1,128)S(1)}, u32[]{:S(2)}, u32[]{:S(2)}) async-start(f32[4,1,1152]{2,1,0:T(1,128)} %copy.150), calls=%async_computation | async-start | bytes 36864 | tf_op jit(solution)/shard_map/all_to_all | solution.py:238
  26.0 88.4 %reduce-scatter.5.cloned.1.call-start = ((), (), s32[]{:S(2)}) async-start(), calls=%async_computation.8 | async-start | bytes 983040 | tf_op jit(solution)/shard_map/reduce_scatter | solution.py:148
  29.8 50.1 %copy-start.104 = (f32[1536]{0:T(1024)}, f32[1536]{0:T(1024)S(1)}, u32[]{:S(2)}) copy-start(f32[1536]{0:T(1024)S(1)} %get-tuple-element.131) | copy-start | bytes 18436
  63.5 50.9 %copy-start.20 = (bf16[256,384]{1,0:T(8,128)(2,1)}, bf16[256,384]{1,0:T(8,128)(2,1)S(1)}, u32[]{:S(2)}) copy-start(bf16[256,384]{1,0:T(8,128)(2,1)S(1)} %get-tuple-element.183) | copy-start | bytes 589828
  63.8 50.6 %copy-start.100 = (f32[384]{0:T(512)}, f32[384]{0:T(512)S(1)}, u32[]{:S(2)}) copy-start(f32[384]{0:T(512)S(1)} %get-tuple-element.244) | copy-start | bytes 4612
  84.5 169.6 %copy-start.76 = (f32[1024,1]{0,1:T(1,128)}, f32[1024,1]{0,1:T(1,128)S(1)}, u32[]{:S(2)}) copy-start(f32[1024,1]{0,1:T(1,128)S(1)} %constant_dynamic-slice_fusion.1) | copy-start | bytes 12292
  87.6 104.0 %reduce-scatter.9.cloned.1.call-start = ((), (), s32[]{:S(2)}) async-start(), calls=%async_computation.10 | async-start | bytes 983040 | tf_op jit(solution)/shard_map/reduce_scatter | solution.py:190
  109.8 66.3 %copy-start.11 = (bf16[1024,384]{1,0:T(8,128)(2,1)}, bf16[1024,384]{1,0:T(8,128)(2,1)S(1)}, u32[]{:S(2)}) copy-start(bf16[1024,384]{1,0:T(8,128)(2,1)S(1)} %all_gather.26) | copy-start | bytes 2359300
  119.4 105.5 %copy-start.83 = (f32[256]{0:T(256)}, f32[256]{0:T(256)S(1)}, u32[]{:S(2)}) copy-start(f32[256]{0:T(256)S(1)} %add_rsqrt_fusion.1) | copy-start | bytes 3076
  126.2 44.6 %copy-start.5 = (bf16[256,384]{1,0:T(8,128)(2,1)}, bf16[256,384]{1,0:T(8,128)(2,1)S(1)}, u32[]{:S(2)}) copy-start(bf16[256,384]{1,0:T(8,128)(2,1)S(1)} %fusion.160) | copy-start | bytes 589828
  167.3 23.2 %all-to-all-start.1 = ((bf16[4,2,128]{2,1,0:T(2,128)(2,1)}), bf16[4,2,128]{2,1,0:T(2,128)(2,1)S(1)}, u32[]{:S(2)}, u32[]{:S(2)}) async-start(bf16[4,2,128]{2,1,0:T(2,128)(2,1)} %reshape.371), calls=%async_computation.3 | async-start | bytes 4096 | tf_op jit(solution)/shard_map/all_to_all | solution.py:171
  170.5 38.7 %reduce-scatter.7.cloned.1.call-start = ((), (), s32[]{:S(2)}) async-start(), calls=%async_computation.9 | async-start | bytes 983040 | tf_op jit(solution)/shard_map/reduce_scatter | solution.py:148
  270.8 21.5 %all-to-all-start.2 = ((bf16[4,2,128]{2,1,0:T(2,128)(2,1)}), bf16[4,2,128]{2,1,0:T(2,128)(2,1)}, u32[]{:S(2)}, u32[]{:S(2)}) async-start(bf16[4,2,128]{2,1,0:T(2,128)(2,1)} %reshape.373), calls=%async_computation.5 | async-start | bytes 4096 | tf_op jit(solution)/shard_map/all_to_all | solution.py:171
  274.6 27.5 %reduce-scatter.11.cloned.1.call-start = ((), (), s32[]{:S(2)}) async-start(), calls=%async_computation.11 | async-start | bytes 983040 | tf_op jit(solution)/shard_map/reduce_scatter | solution.py:190
  275.2 197.9 %all-reduce.14.cloned.1.call-start = ((), (), s32[]{:S(2)}) async-start(), calls=%async_computation.14 | async-start | bytes 9437184 | tf_op jit(solution)/shard_map/psum | solution.py:320
  313.8 8.3 %all-to-all-start.3 = ((f32[4,1,1152]{2,1,0:T(1,128)}), f32[4,1,1152]{2,1,0:T(1,128)S(1)}, u32[]{:S(2)}, u32[]{:S(2)}) async-start(f32[4,1,1152]{2,1,0:T(1,128)} %all_to_all.26), calls=%async_computation.7 | async-start | bytes 36864 | tf_op jit(solution)/shard_map/all_to_all | solution.py:302
  317.1 163.1 %all-reduce.12.cloned.1.call-start = ((), (), s32[]{:S(2)}) async-start(), calls=%async_computation.13 | async-start | bytes 3305472 | tf_op jit(solution)/shard_map/psum | solution.py:320
  334.5 357.1 %all-reduce.10.cloned.1.call-start = ((), (), s32[]{:S(2)}) async-start(), calls=%async_computation.12 | async-start | bytes 23592960 | tf_op jit(solution)/shard_map/psum | solution.py:320
  341.0 44.9 %copy-start.4 = (bf16[1024,384]{1,0:T(8,128)(2,1)S(1)}, bf16[1024,384]{1,0:T(8,128)(2,1)}, u32[]{:S(2)}) copy-start(bf16[1024,384]{1,0:T(8,128)(2,1)} %copy-done.2) | copy-start | bytes 2359300
  341.0 44.9 %copy-start.77 = (f32[1024,1]{0,1:T(1,128)S(1)}, f32[1024,1]{0,1:T(1,128)}, u32[]{:S(2)}) copy-start(f32[1024,1]{0,1:T(1,128)} %copy-done.76) | copy-start | bytes 12292
  341.0 69.8 %copy-start.111 = (bf16[384]{0:T(512)(128)(2,1)S(1)}, bf16[384]{0:T(512)(128)(2,1)}, u32[]{:S(2)}) copy-start(bf16[384]{0:T(512)(128)(2,1)} %get-tuple-element.176) | copy-start | bytes 2308
  341.0 71.0 %copy-start.107 = (bf16[3072]{0:T(1024)(128)(2,1)S(1)}, bf16[3072]{0:T(1024)(128)(2,1)}, u32[]{:S(2)}) copy-start(bf16[3072]{0:T(1024)(128)(2,1)} %get-tuple-element.236) | copy-start | bytes 18436
  341.6 71.2 %copy-start.88 = (f32[256]{0:T(256)S(1)}, f32[256]{0:T(256)}, u32[]{:S(2)}) copy-start(f32[256]{0:T(256)} %copy-done.87) | copy-start | bytes 3076
  341.6 71.4 %copy-start.112 = (bf16[384]{0:T(512)(128)(2,1)S(1)}, bf16[384]{0:T(512)(128)(2,1)}, u32[]{:S(2)}) copy-start(bf16[384]{0:T(512)(128)(2,1)} %get-tuple-element.174) | copy-start | bytes 2308
  (120 other events, 1100.1 us)
Sparse Core Ops, SparseCore 0:
  87.7 26.5 reduce-scatter.4
  160.8 22.8 reduce-scatter.8
  186.6 22.5 reduce-scatter.6
  277.4 24.6 reduce-scatter.10
  305.9 87.6 all-reduce.13
  396.6 62.6 all-reduce.11
  466.8 224.7 all-reduce.9
